TPU v7x, 512 devices: a whole 4x4x16 slice. The times are simulated.
512 devices in a mesh: seq: 64 (over z, x), head: 8 (over y, core).
Axes of the slice: x: 4, y: 4, z: 16, core: 2. Of those that a mesh axis runs over, the one named last changes fastest.
Arguments:
- queries: bfloat16 [2, 8192, 16, 128], P(None, 'seq', 'head'), may hold values from -6 to 6
- keys: bfloat16 [2, 8192, 16, 128], P(None, 'seq', 'head'), may hold values from -6 to 6
- values: bfloat16 [2, 8192, 16, 128], P(None, 'seq', 'head'), may hold values from -6 to 6
- teacher: bfloat16 [2, 8192, 16, 128], P(None, 'seq', 'head'), may hold values from -4 to 4
- query_map: bfloat16 [128, 128], replicated, may hold values from -1.5 to 1.5
- key_map: bfloat16 [128, 128], replicated, may hold values from -1.5 to 1.5
Outputs:
- grad_query_map: float32 [128, 128], replicated
- grad_key_map: float32 [128, 128], replicated
All inputs are finite; a program needn't handle non-finite values.
Results may differ from a plain program's by a relative error of at most 0.0003.
Values sent between devices are 32-bit elements; how exact they have to be, the bound alone decides.
A program may use at most 128 MiB of HBM per device.

v0:
```python
import jax
import jax.numpy as jnp
from jax import lax
from jax.sharding import PartitionSpec as P

HIGH = lax.Precision.HIGHEST


def entering(part, axis, combine, identity, reverse):
    count = lax.axis_size(axis)
    place = lax.axis_index(axis)
    ahead = count - 1 - place if reverse else place
    gathered = jax.tree.map(lambda a: lax.all_gather(a, axis), part)
    state = jax.tree.map(lambda a, e: jnp.zeros_like(a) + jnp.asarray(e, a.dtype), part, identity)

    def one(step, state):
        source = count - 1 - step if reverse else step
        return combine(
            state, jax.tree.map(lambda a: lax.dynamic_index_in_dim(a, source, 0, False), gathered)
        )

    return lax.fori_loop(0, ahead, one, state)


def feature(inputs, matrix):
    logits = jnp.dot(inputs, matrix, preferred_element_type=jnp.float32)
    rising = jnp.exp(logits)
    falling = jnp.exp(-logits)
    return jnp.concatenate(
        [
            rising / jnp.sum(rising, -1, keepdims=True),
            falling / jnp.sum(falling, -1, keepdims=True),
        ],
        -1,
    )


def feature_back(phi, dphi):
    half_width = phi.shape[-1] // 2
    part_up = phi[..., :half_width]
    part_down = phi[..., half_width:]
    grad_up = dphi[..., :half_width]
    grad_down = dphi[..., half_width:]
    return part_up * (grad_up - jnp.sum(part_up * grad_up, -1, keepdims=True)) - part_down * (
        grad_down - jnp.sum(part_down * grad_down, -1, keepdims=True)
    )


def add_pair(earlier, later):
    return (earlier[0] + later[0], earlier[1] + later[1])


def per_device(queries, keys, values, teacher, query_map, key_map):
    query_phi = feature(queries, query_map)
    key_phi = feature(keys, key_map)
    value_full = values.astype(jnp.float32)
    target_full = teacher.astype(jnp.float32)
    size_t = queries.shape[1]
    causal = (
        lax.broadcasted_iota(jnp.int32, (size_t, size_t), 0)
        >= lax.broadcasted_iota(jnp.int32, (size_t, size_t), 1)
    ).astype(jnp.float32)
    local_state = jnp.einsum("bthf,bthd->bhfd", key_phi, value_full, precision=HIGH)
    local_norm = jnp.sum(key_phi, 1)
    zero_pair = (jnp.zeros_like(local_state), jnp.zeros_like(local_norm))
    prefix_state, prefix_norm = entering(
        (local_state, local_norm), "seq", add_pair, zero_pair, False
    )
    scores = jnp.einsum("bihf,bjhf->bhij", query_phi, key_phi, precision=HIGH) * causal
    numerator = jnp.einsum("bhij,bjhd->bihd", scores, value_full, precision=HIGH) + jnp.einsum(
        "bihf,bhfd->bihd", query_phi, prefix_state, precision=HIGH
    )
    denominator = jnp.transpose(jnp.sum(scores, 3), (0, 2, 1)) + jnp.einsum(
        "bihf,bhf->bih", query_phi, prefix_norm, precision=HIGH
    )
    output = numerator / denominator[..., None]
    misfit = output - target_full
    grad_num = misfit / denominator[..., None]
    grad_den = -jnp.sum(misfit * output, 3) / denominator
    mixed_grad = (
        jnp.einsum("bihd,bjhd->bhij", grad_num, value_full, precision=HIGH)
        + jnp.transpose(grad_den, (0, 2, 1))[..., None]
    ) * causal
    query_dphi = (
        jnp.einsum("bhij,bjhf->bihf", mixed_grad, key_phi, precision=HIGH)
        + jnp.einsum("bihd,bhfd->bihf", grad_num, prefix_state, precision=HIGH)
        + grad_den[..., None] * prefix_norm[:, None]
    )
    grad_q = jnp.einsum(
        "bthd,bthf->df",
        queries.astype(jnp.float32),
        feature_back(query_phi, query_dphi),
        precision=HIGH,
    )
    back_state = jnp.einsum("bihf,bihd->bhfd", query_phi, grad_num, precision=HIGH)
    back_norm = jnp.einsum("bihf,bih->bhf", query_phi, grad_den, precision=HIGH)
    suffix_state, suffix_norm = entering((back_state, back_norm), "seq", add_pair, zero_pair, True)
    key_dphi = (
        jnp.einsum("bhij,bihf->bjhf", mixed_grad, query_phi, precision=HIGH)
        + jnp.einsum("bjhd,bhfd->bjhf", value_full, suffix_state, precision=HIGH)
        + suffix_norm[:, None]
    )
    grad_k = jnp.einsum(
        "bthd,bthf->df", keys.astype(jnp.float32), feature_back(key_phi, key_dphi), precision=HIGH
    )
    grad_q, grad_k = lax.psum((grad_q, grad_k), ("seq", "head"))
    return (grad_q, grad_k)


def solution(mesh):
    in_specs = (
        P(None, "seq", "head", None),
        P(None, "seq", "head", None),
        P(None, "seq", "head", None),
        P(None, "seq", "head", None),
        P(),
        P(),
    )
    out_specs = (P(), P())
    return jax.shard_map(
        per_device, mesh=mesh, in_specs=in_specs, out_specs=out_specs, check_vma=False
    )
```

profile of v0, /device:TPU:1, one launch (start us, length us, event | category | flops | bytes accessed | tf_op | source)
XLA Modules:
  0.0 1198.4 jit_solution(1929712847162049316)
XLA Ops:
  7.2 1.2 exponential_reduce_fusion
  8.5 1.2 exponential_reduce_fusion.1
  9.8 1.2 fusion.24
  12.4 79.1 %all-gather.1 = f32[128,2,256]{2,1,0:T(2,128)S(1)} all-gather(f32[2,2,256]{2,1,0:T(2,128)S(1)} %fusion.23), channel_id=3, replica_groups=mesh['seq'=64,'head'=8] {'seq'}, dimensions={0}, use_global_device_ids=true | all-gather | bytes 266240 | tf_op jit(solution)/shard_map/all_gather | solution.py:13
  92.6 218.1 %all-gather.7.cloned.1.call-done = f32[128,2,256,128]{3,2,1,0:T(8,128)} async-done(((f32[2,2,256,128]{3,2,1,0:T(8,128)}), f32[128,2,256,128]{3,2,1,0:T(8,128)}) %all-gather.7.cloned.1.call-update) | async-done | bytes 33554448 | tf_op jit(solution)/shard_map/all_gather | solution.py:13
  312.5 1.4 fusion.45
  314.6 143.2 %all-gather.3 = f32[128,2,256]{2,1,0:T(2,128)S(1)} all-gather(f32[2,2,256]{2,1,0:T(2,128)S(1)} %bitcast.86), channel_id=5, replica_groups=mesh['seq'=64,'head'=8] {'seq'}, dimensions={0}, use_global_device_ids=true | all-gather | bytes 266240 | tf_op jit(solution)/shard_map/all_gather | solution.py:13
  459.5 1.8 convolution_bitcast_fusion.3
  461.9 211.4 %all-gather.9.cloned.1.call-done = f32[128,2,256,128]{3,2,1,0:T(8,128)} async-done(((f32[2,2,256,128]{3,2,1,0:T(8,128)}), f32[128,2,256,128]{3,2,1,0:T(8,128)}) %all-gather.9.cloned.1.call-update) | async-done | bytes 33554448 | tf_op jit(solution)/shard_map/all_gather | solution.py:13
  673.4 75.6 %while.27 = (s32[]{:T(128)}, f32[2,2,256,128]{3,2,1,0:T(8,128)S(1)}, f32[2,2,256]{2,1,0:T(2,128)S(1)}, s32[]{:T(128)}, f32[64,2,2,256,128]{4,3,2,1,0:T(8,128)}, ...) while((s32[]{:T(128)}, f32[2,2,256,128]{3,2,1,0:T(8,128)S(1)}, ...), condition=%wide.region_13.14_spmd, body=%wide.region_12.13_spmd.sunk | while | flops 132102 | bytes 1585315 | solution.py:22
  673.4 1.2 bitcast_add_fusion.10
  674.6 1.2 bitcast_add_fusion.10
  675.8 1.2 bitcast_add_fusion.10
  677.0 1.2 bitcast_add_fusion.10
  678.2 1.2 bitcast_add_fusion.10
  679.4 1.2 bitcast_add_fusion.10
  680.6 1.2 bitcast_add_fusion.10
  681.8 1.2 bitcast_add_fusion.10
  683.0 1.2 bitcast_add_fusion.10
  684.2 1.2 bitcast_add_fusion.10
  685.4 1.2 bitcast_add_fusion.10
  686.6 1.2 bitcast_add_fusion.10
  687.8 1.2 bitcast_add_fusion.10
  689.0 1.2 bitcast_add_fusion.10
  690.2 1.2 bitcast_add_fusion.10
  691.4 1.2 bitcast_add_fusion.10
  692.6 1.2 bitcast_add_fusion.10
  693.8 1.2 bitcast_add_fusion.10
  695.0 1.2 bitcast_add_fusion.10
  696.2 1.2 bitcast_add_fusion.10
  697.4 1.2 bitcast_add_fusion.10
  698.6 1.2 bitcast_add_fusion.10
  699.8 1.2 bitcast_add_fusion.10
  701.0 1.2 bitcast_add_fusion.10
  702.2 1.2 bitcast_add_fusion.10
  703.4 1.2 bitcast_add_fusion.10
  704.6 1.2 bitcast_add_fusion.10
  705.8 1.2 bitcast_add_fusion.10
  707.0 1.2 bitcast_add_fusion.10
  708.2 1.2 bitcast_add_fusion.10
  709.4 1.2 bitcast_add_fusion.10
  710.6 1.2 bitcast_add_fusion.10
  711.8 1.2 bitcast_add_fusion.10
  713.0 1.2 bitcast_add_fusion.10
  714.2 1.2 bitcast_add_fusion.10
  715.4 1.2 bitcast_add_fusion.10
  716.6 1.2 bitcast_add_fusion.10
  717.8 1.2 bitcast_add_fusion.10
  720.2 1.2 bitcast_add_fusion.10
  721.4 1.2 bitcast_add_fusion.10
  723.8 1.2 bitcast_add_fusion.10
  725.0 1.2 bitcast_add_fusion.10
  728.6 1.2 bitcast_add_fusion.10
  732.2 1.2 bitcast_add_fusion.10
  735.8 1.2 bitcast_add_fusion.10
  739.4 1.2 bitcast_add_fusion.10
  740.6 1.2 bitcast_add_fusion.10
  743.0 1.2 bitcast_add_fusion.10
  744.2 1.2 bitcast_add_fusion.10
  746.6 1.2 bitcast_add_fusion.10
  747.8 1.2 bitcast_add_fusion.10
  750.4 438.3 %all-reduce.3.cloned.1.call-done = (f32[128,128]{0,1:T(8,128)}, f32[128,128]{0,1:T(8,128)}) async-done(((f32[128,128]{0,1:T(8,128)}, f32[128,128]{0,1:T(8,128)}), (f32[128,128]{0,1:T(8,128)}, f32[128,128]{0,1:T(8,128)})) %all-reduce.3.cloned.1.call-update) | async-done | bytes 131088 | tf_op jit(solution)/shard_map/psum | solution.py:106
  1188.8 1.6 copy.54
  1190.3 1.6 copy.55
  (111 shorter events, 23.7 us)
Async XLA Ops:
  7.2 2.7 copy-start
  7.2 742.3 %copy-start.1 = (bf16[2,128,2,128]{3,2,1,0:T(2,128)(2,1)S(1)}, bf16[2,128,2,128]{3,2,1,0:T(2,128)(2,1)}, u32[]{:S(2)}) copy-start(bf16[2,128,2,128]{3,2,1,0:T(2,128)(2,1)} %param.11) | copy-start | bytes 393220
  7.2 303.5 %all-gather.7.cloned.1.call-start = ((), (), s32[]{:S(2)}) async-start(), calls=%async_computation | async-start | bytes 34078720 | tf_op jit(solution)/shard_map/all_gather | solution.py:13
  11.0 662.3 %all-gather.9.cloned.1.call-start = ((), (), s32[]{:S(2)}) async-start(), calls=%async_computation.1 | async-start | bytes 34078720 | tf_op jit(solution)/shard_map/all_gather | solution.py:13
  314.0 874.8 %all-reduce.3.cloned.1.call-start = ((), (), s32[]{:S(2)}) async-start(), calls=%async_computation.2 | async-start | bytes 262144 | tf_op jit(solution)/shard_map/psum | solution.py:106
Sparse Core Ops, SparseCore 0:
  11.2 299.4 all-gather.6
  314.1 359.2 all-gather.8
  750.6 438.1 all-reduce.2
where the time goes:
time: 1200 us
  waiting for transfers between devices  868 us (72%)
  blocking collectives  222 us (18%)
  other arithmetic  74.4 us (6%)
  between operations  13.9 us (1%)
  matrix products  13.8 us (1%)
    psum x1, waiting for transfers between devices, per_device(): grad_q, grad_k = lax.psum((grad_q, grad_k), ('seq', 'head'))  438 us
    all_gather x2, waiting for transfers between devices, entering(): gathered = jax.tree.map(lambda a: lax.all_gather(a, axis), part)  430 us
    all_gather x2, blocking collectives, entering(): gathered = jax.tree.map(lambda a: lax.all_gather(a, axis), part)  222 us
    add x126, other arithmetic, add_pair(): return (earlier[0] + later[0], earlier[1] + later[1])  73.9 us
  transfers between devices with their start and end apart: 3, of which 3 were waited for; matrix products, arithmetic and copies ran while one was open for 1% of the time, Pallas kernels for 0%

commit v1 on v0

v1 whole, which is shorter than its diff:
```python
import jax
import jax.numpy as jnp
from jax import lax
from jax.experimental import pallas as pl
from jax.experimental.pallas import tpu as pltpu
from jax.sharding import PartitionSpec as P

MESH = pl.DeviceIdType.MESH
F32 = jnp.float32
BF16 = jnp.bfloat16

NZ, NX, NY, NC = 16, 4, 4, 2
TOK = 128
DH = 128
F2 = 256
LOC = NX * TOK
FC = F2 // NZ
Z_FAR_FIRST = (8, 7, 9, 6, 10, 5, 11, 4, 12, 3, 13, 2, 14, 1, 15)
X_FAR_FIRST = (2, 1, 3)
XY_FAR_FIRST = tuple(
    sorted(
        ((dx, dy) for dx in range(NX) for dy in range(NY) if dx or dy),
        key=lambda d: -(min(d[0], NX - d[0]) + min(d[1], NY - d[1])),
    )
)

NN = (((1,), (0,)), ((), ()))
NT = (((1,), (1,)), ((), ()))
TN = (((0,), (0,)), ((), ()))


def split(a):
    high = a.astype(BF16)
    return high, (a - high.astype(F32)).astype(BF16)


def mm(a, b, dims):
    return lax.dot_general(a, b, dims, preferred_element_type=F32)


def mm3(a, b, dims):
    return mm(a[0], b[0], dims) + (mm(a[0], b[1], dims) + mm(a[1], b[0], dims))


def mm2(a, b, dims):
    return mm(a[0], b, dims) + mm(a[1], b, dims)


def feature(inputs, matrix):
    logits = mm(inputs, matrix, NN)
    rising = jnp.exp(logits)
    falling = jnp.exp(-logits)
    return jnp.concatenate(
        [
            rising / jnp.sum(rising, -1, keepdims=True),
            falling / jnp.sum(falling, -1, keepdims=True),
        ],
        -1,
    )


def feature_back(phi, dphi):
    half = phi.shape[-1] // 2
    up, down = phi[:, :half], phi[:, half:]
    grad_up, grad_down = dphi[:, :half], dphi[:, half:]
    return up * (grad_up - jnp.sum(up * grad_up, -1, keepdims=True)) - down * (
        grad_down - jnp.sum(down * grad_down, -1, keepdims=True)
    )


def kernel(
    k_hbm,
    v_hbm,
    q_hbm,
    t_hbm,
    qmap_hbm,
    kmap_hbm,
    out_ref,
    raw,
    maps,
    wide,
    stage,
    held,
    state,
    norms,
    got_state,
    got_norm,
    totals,
    entering,
    part,
    got_part,
    sums,
    got_sum,
    got_core,
    load_sem,
    x_send,
    x_recv,
    z_send,
    z_recv,
    n_send,
    n_recv,
    r_send,
    r_recv,
    c_send,
    c_recv,
    g_send,
    g_recv,
):
    seq, head = lax.axis_index("seq"), lax.axis_index("head")
    z, x = seq // NX, seq % NX
    y, core = head // NC, head % NC

    def at_z(d):
        other = (z + d) % NZ
        return other, (other * NX + x, head)

    def at_x(d):
        other = (x + d) % NX
        return other, (z * NX + other, head)

    def at_xy(d):
        ox, oy = (x + d[0]) % NX, (y + d[1]) % NY
        return ox * NY + oy, (z * NX + ox, oy * NC + core)

    other_core = (seq, y * NC + (1 - core))

    loads = []
    for i, (src, dst) in enumerate(
        (
            (k_hbm, raw.at[0]),
            (v_hbm, raw.at[1]),
            (kmap_hbm, maps.at[0]),
            (q_hbm, raw.at[2]),
            (t_hbm, raw.at[3]),
            (qmap_hbm, maps.at[1]),
        )
    ):
        load = pltpu.make_async_copy(src, dst, load_sem.at[i])
        load.start()
        loads.append(load)

    barrier = pltpu.get_barrier_semaphore()
    partners = [at_x(d)[1] for d in X_FAR_FIRST]
    partners += [at_z(d)[1] for d in Z_FAR_FIRST]
    partners += [at_xy(d)[1] for d in XY_FAR_FIRST if d[1]]
    partners += [other_core]
    for partner in partners:
        pl.semaphore_signal(barrier, inc=1, device_id=partner, device_id_type=MESH)

    sent = []

    def send(src, dst, send_sem, recv_sem, device):
        copy = pltpu.make_async_remote_copy(
            src_ref=src,
            dst_ref=dst,
            send_sem=send_sem,
            recv_sem=recv_sem,
            device_id=device,
            device_id_type=MESH,
        )
        copy.start()
        sent.append(copy)
        return copy

    def widen(i):
        wide[i] = raw[i].astype(F32)
        for b in range(2):
            for h in range(2):
                stage[i, b * 2 + h] = wide[i, pl.ds(b * 2 * TOK + h, TOK, stride=2), :]
        held[i, x] = stage[i, x]

    loads[0].wait()
    widen(0)
    loads[1].wait()
    widen(1)
    pl.semaphore_wait(barrier, len(partners))

    x_copies = [[], [], [], []]

    def send_x(i):
        for d in X_FAR_FIRST:
            other, device = at_x(d)
            x_copies[i].append(
                send(stage.at[i, other], held.at[i, x], x_send.at[i, d - 1], x_recv.at[i, d - 1], device)
            )

    send_x(0)
    send_x(1)
    loads[3].wait()
    widen(2)
    send_x(2)
    loads[4].wait()
    widen(3)
    send_x(3)
    loads[2].wait()
    loads[5].wait()

    def receive_x(i):
        for copy in x_copies[i]:
            copy.wait_recv()
        return held[i].reshape(LOC, DH)

    def scatter_z(scan, full_state, full_norm):
        state[scan] = full_state.reshape(NZ, FC, DH)
        norms[scan] = full_norm
        copies = []
        for d in Z_FAR_FIRST:
            other, device = at_z(d)
            copies.append(
                send(state.at[scan, other], got_state.at[scan, z], z_send.at[2 * scan, d - 1], z_recv.at[2 * scan, d - 1], device)
            )
            copies.append(
                send(norms.at[scan], got_norm.at[scan, z], n_send.at[scan, d - 1], n_recv.at[scan, d - 1], device)
            )
        got_state[scan, z] = state[scan, z]
        got_norm[scan, z] = norms[scan]
        return copies

    def return_z(scan, copies, reverse):
        for copy in copies:
            copy.wait_recv()
        order = range(NZ - 1, -1, -1) if reverse else range(NZ)
        running = jnp.zeros((FC, DH), F32)
        for one in order:
            totals[scan, one] = running
            running = running + got_state[scan, one]
        copies = []
        for d in Z_FAR_FIRST:
            other, device = at_z(d)
            copies.append(
                send(totals.at[scan, other], entering.at[scan, z], z_send.at[2 * scan + 1, d - 1], z_recv.at[2 * scan + 1, d - 1], device)
            )
        entering[scan, z] = totals[scan, z]
        norm = jnp.zeros((1, F2), F32)
        for one in order:
            before = one > z if reverse else one < z
            norm = norm + jnp.where(before, got_norm[scan, one], 0.0)
        return copies, norm

    def receive_z(scan, copies):
        for copy in copies:
            copy.wait_recv()
        return entering[scan].reshape(F2, DH)

    keys = receive_x(0).astype(BF16)
    key_phi = feature(keys, maps[0])
    kphi = split(key_phi)
    values = receive_x(1).astype(BF16)
    copies = scatter_z(0, mm2(kphi, values, TN), jnp.sum(key_phi, 0, keepdims=True))

    queries = receive_x(2).astype(BF16)
    query_phi = feature(queries, maps[1])
    qphi = split(query_phi)
    causal = lax.broadcasted_iota(jnp.int32, (LOC, LOC), 0) >= lax.broadcasted_iota(
        jnp.int32, (LOC, LOC), 1
    )
    scores = jnp.where(causal, mm3(qphi, kphi, NT), 0.0)
    inner_num = mm2(split(scores), values, NN)
    inner_den = jnp.sum(scores, 1, keepdims=True)
    target = receive_x(3)

    copies, prefix_norm = return_z(0, copies, False)
    denominator = inner_den + jnp.sum(query_phi * prefix_norm, 1, keepdims=True)
    prefix = split(receive_z(0, copies))

    output = (inner_num + mm3(qphi, prefix, NN)) / denominator
    misfit = output - target
    grad_num = misfit / denominator
    grad_den = -jnp.sum(misfit * output, 1, keepdims=True) / denominator
    gnum = split(grad_num)
    copies = scatter_z(
        1, mm3(qphi, gnum, TN), jnp.sum(query_phi * grad_den, 0, keepdims=True)
    )

    mixed = split(jnp.where(causal, mm(gnum[0], values, NT) + mm(gnum[1], values, NT) + grad_den, 0.0))
    query_dphi = mm3(mixed, kphi, NN) + mm3(gnum, prefix, NT) + grad_den * prefix_norm
    key_inner = mm3(mixed, qphi, TN)
    grad_aq = split(feature_back(query_phi, query_dphi))
    grad_q = mm(queries, grad_aq[0], TN) + mm(queries, grad_aq[1], TN)
    part[:, 0] = grad_q.reshape(16, 8, DH)

    copies, suffix_norm = return_z(1, copies, True)
    suffix = split(receive_z(1, copies))
    key_dphi = key_inner + mm(values, suffix[0], NT) + mm(values, suffix[1], NT) + suffix_norm
    grad_ak = split(feature_back(key_phi, key_dphi))
    grad_k = mm(keys, grad_ak[0], TN) + mm(keys, grad_ak[1], TN)
    part[:, 1] = grad_k.reshape(16, 8, DH)

    mine = x * NY + y
    copies = []
    for i, d in enumerate(XY_FAR_FIRST):
        other, device = at_xy(d)
        copies.append(send(part.at[other], got_part.at[mine], r_send.at[i], r_recv.at[i], device))
    got_part[mine] = part[mine]
    for copy in copies:
        copy.wait_recv()
    sums[0] = jnp.sum(got_part[...], 0)
    copy = send(sums.at[0], got_core, c_send.at[0], c_recv.at[0], other_core)
    copy.wait_recv()
    sums[1] = sums[0] + got_core[...]
    copies = []
    for d in Z_FAR_FIRST:
        other, device = at_z(d)
        copies.append(send(sums.at[1], got_sum.at[z], r_send.at[14 + d], r_recv.at[14 + d], device))
    got_sum[z] = sums[1]
    for copy in copies:
        copy.wait_recv()
    sums[2] = jnp.sum(got_sum[...], 0)
    copies = []
    for i, d in enumerate(XY_FAR_FIRST):
        other, device = at_xy(d)
        copies.append(send(sums.at[2], out_ref.at[mine], g_send.at[i], g_recv.at[i], device))
    out_ref[mine] = sums[2]
    for copy in copies:
        copy.wait_recv()
    for copy in sent:
        copy.wait_send()


def per_device(queries, keys, values, teacher, query_map, key_map):
    def flat(a):
        return a.reshape(-1, DH)

    out = pl.pallas_call(
        kernel,
        out_shape=jax.ShapeDtypeStruct((16, 2, 8, DH), F32),
        in_specs=[pl.BlockSpec(memory_space=pl.ANY)] * 6,
        out_specs=pl.BlockSpec(memory_space=pltpu.VMEM),
        scratch_shapes=[
            pltpu.VMEM((4, 4 * TOK, DH), BF16),
            pltpu.VMEM((2, DH, DH), BF16),
            pltpu.VMEM((4, 4 * TOK, DH), F32),
            pltpu.VMEM((4, 4, TOK, DH), F32),
            pltpu.VMEM((4, NX, TOK, DH), F32),
            pltpu.VMEM((2, NZ, FC, DH), F32),
            pltpu.VMEM((2, 1, F2), F32),
            pltpu.VMEM((2, NZ, FC, DH), F32),
            pltpu.VMEM((2, NZ, 1, F2), F32),
            pltpu.VMEM((2, NZ, FC, DH), F32),
            pltpu.VMEM((2, NZ, FC, DH), F32),
            pltpu.VMEM((16, 2, 8, DH), F32),
            pltpu.VMEM((16, 2, 8, DH), F32),
            pltpu.VMEM((3, 2, 8, DH), F32),
            pltpu.VMEM((NZ, 2, 8, DH), F32),
            pltpu.VMEM((2, 8, DH), F32),
            pltpu.SemaphoreType.DMA((6,)),
            pltpu.SemaphoreType.DMA((4, 3)),
            pltpu.SemaphoreType.DMA((4, 3)),
            pltpu.SemaphoreType.DMA((4, 15)),
            pltpu.SemaphoreType.DMA((4, 15)),
            pltpu.SemaphoreType.DMA((2, 15)),
            pltpu.SemaphoreType.DMA((2, 15)),
            pltpu.SemaphoreType.DMA((30,)),
            pltpu.SemaphoreType.DMA((30,)),
            pltpu.SemaphoreType.DMA((1,)),
            pltpu.SemaphoreType.DMA((1,)),
            pltpu.SemaphoreType.DMA((15,)),
            pltpu.SemaphoreType.DMA((15,)),
        ],
        compiler_params=pltpu.CompilerParams(
            collective_id=0, has_side_effects=True, vmem_limit_bytes=56 * 1024 * 1024
        ),
        name="hedgehog",
    )(flat(keys), flat(values), flat(queries), flat(teacher), query_map, key_map)
    return out[:, 0].reshape(DH, DH), out[:, 1].reshape(DH, DH)


def solution(mesh):
    split_spec = P(None, "seq", "head", None)
    return jax.shard_map(
        per_device,
        mesh=mesh,
        in_specs=(split_spec,) * 4 + (P(), P()),
        out_specs=(P(), P()),
        check_vma=False,
    )
```

time: 1200 us -> 87.3 us (0.07)
  waiting for transfers between devices: 868 us -> 0 us
  blocking collectives: 222 us -> 0 us
  Pallas kernels: 0 us -> 84.9 us
  other arithmetic: 74.4 us -> 0 us
  matrix products: 13.8 us -> 0 us
  between operations: 13.9 us -> 0.64 us
    psum x1 -> x0, waiting for transfers between devices: 438 us -> none  [per_device(): grad_q, grad_k = lax.psum((grad_q, grad_k), ('seq', 'head'))]
    all_gather x2 -> x0, waiting for transfers between devices: 430 us -> none  [entering(): gathered = jax.tree.map(lambda a: lax.all_gather(a, axis), part)]
    all_gather x2 -> x0, blocking collectives: 222 us -> none  [entering(): gathered = jax.tree.map(lambda a: lax.all_gather(a, axis), part)]
    pallas_call x0 -> x1, Pallas kernels: none -> 84.9 us  [per_device(): pl.pallas_call(kernel, out_shape=jax.ShapeDtypeStruct((16, 2, 8, DH), F32...]
    add x127 -> x0, other arithmetic: 73.9 us -> none  [the longest x126 73.9 us: add_pair(): return (earlier[0] + later[0], earlier[1] + later[1])]
    dot_general x16 -> x0, matrix products: 13.8 us -> none  [the longest x2 2.43 us: feature(): logits = jnp.dot(inputs, matrix, preferred_element_type=jnp.float32)]
  transfers between devices with their start and end apart: 3 -> 0, of which waited for: 3 -> 0; matrix products, arithmetic and copies ran while one was open for 1% -> 0% of each run, Pallas kernels for 0% -> 0%
where the time goes in v1:
time: 87.3 us; the launch traced here: 87.1 us
  Pallas kernels  84.9 us (97%)
  local copies, waits for them, and re-layouts  1.53 us (2%)
    pallas_call x1, Pallas kernels, per_device(): pl.pallas_call(kernel, out_shape=jax.ShapeDtypeStruct((16, 2, 8, DH), F32...  84.9 us

profile of v1, /device:TPU:1, one launch (start us, length us, event | category | flops | bytes accessed | tf_op | source)
XLA Modules:
  0.0 87.1 jit_solution(18226184641032560328)
XLA Ops:
  0.6 84.9 %hedgehog.1 = f32[16,2,8,128]{3,2,1,0:T(8,128)} custom-call(bf16[512,128]{1,0:T(8,128)(2,1)} %bitcast.8, bf16[512,128]{1,0:T(8,128)(2,1)} %bitcast.9, bf16[512,128]{1,0:T(8,128)(2,1)} %bitcast.10, bf16[512,128]{1,0:T(8,128)(2,1)} %bitcast.11, bf16[128,128]{1,0:T(8,128)(2,1)} %qmap_hbm.1, bf16[128,128]{1,0:T(8,128)(2,1)} %kmap_hbm.1), custom_call_target="tpu_custom_call" | custom-call | tf_op jit(solution)/shard_map/hedgehog/pallas_call | solution.py:324
  85.6 1.5 %slice_bitcast_fusion = (f32[128,128]{1,0:T(8,128)}, f32[128,128]{1,0:T(8,128)}) fusion(f32[16,2,8,128]{3,2,1,0:T(8,128)} %hedgehog.1), kind=kLoop, calls=%fused_computation | loop fusion | bytes 262144 | tf_op jit(solution)/shard_map/reshape;squeeze | solution.py:365

commit v2 on v1

v2 whole, which is shorter than its diff:
```python
import jax
import jax.numpy as jnp
from jax import lax
from jax.experimental import pallas as pl
from jax.experimental.pallas import tpu as pltpu
from jax.sharding import PartitionSpec as P

MESH = pl.DeviceIdType.MESH
F32 = jnp.float32
BF16 = jnp.bfloat16

NZ, NX, NY, NC = 16, 4, 4, 2
TOK = 128
DH = 128
F2 = 256
LOC = NX * TOK
FC = F2 // NZ
Z_FAR_FIRST = (8, 7, 9, 6, 10, 5, 11, 4, 12, 3, 13, 2, 14, 1, 15)
X_FAR_FIRST = (2, 1, 3)
PLANE_FAR_FIRST = tuple(
    sorted(
        ((dx, dy, dc) for dx in range(NX) for dy in range(NY) for dc in range(NC) if dx or dy or dc),
        key=lambda d: -(min(d[0], NX - d[0]) + min(d[1], NY - d[1])),
    )
)
NP = NX * NY
ROWS = FC + 2

NN = (((1,), (0,)), ((), ()))
NT = (((1,), (1,)), ((), ()))
TN = (((0,), (0,)), ((), ()))


def split(a):
    high = a.astype(BF16)
    return high, (a - high.astype(F32)).astype(BF16)


def mm(a, b, dims):
    return lax.dot_general(a, b, dims, preferred_element_type=F32)


def mm3(a, b, dims):
    return mm(a[0], b[0], dims) + (mm(a[0], b[1], dims) + mm(a[1], b[0], dims))


def mm2(a, b, dims):
    return mm(a[0], b, dims) + mm(a[1], b, dims)


def feature(inputs, matrix):
    logits = mm(inputs, matrix, NN)
    rising = jnp.exp(logits)
    falling = jnp.exp(-logits)
    return jnp.concatenate(
        [
            rising / jnp.sum(rising, -1, keepdims=True),
            falling / jnp.sum(falling, -1, keepdims=True),
        ],
        -1,
    )


def feature_back(phi, dphi):
    half = phi.shape[-1] // 2
    up, down = phi[:, :half], phi[:, half:]
    grad_up, grad_down = dphi[:, :half], dphi[:, half:]
    return up * (grad_up - jnp.sum(up * grad_up, -1, keepdims=True)) - down * (
        grad_down - jnp.sum(down * grad_down, -1, keepdims=True)
    )


def kernel(
    k_hbm,
    v_hbm,
    q_hbm,
    t_hbm,
    qmap_hbm,
    kmap_hbm,
    out_ref,
    raw,
    maps,
    wide,
    stage,
    held,
    state,
    got_state,
    totals,
    entering,
    part,
    got_part,
    sums,
    got_sum,
    load_sem,
    x_send,
    x_recv,
    z_send,
    z_recv,
    r_send,
    r_recv,
    s_send,
    s_recv,
    g_send,
    g_recv,
    own_sem,
    near_sem,
    far_sem,
    row_sem,
    plane_sem,
):
    seq, head = lax.axis_index("seq"), lax.axis_index("head")
    z, x = seq // NX, seq % NX
    y, core = head // NC, head % NC

    def at_z(d):
        other = (z + d) % NZ
        return other, (other * NX + x, head)

    def at_x(d):
        other = (x + d) % NX
        return other, (z * NX + other, head)

    def at_plane(d):
        ox, oy, oc = (x + d[0]) % NX, (y + d[1]) % NY, (core + d[2]) % NC
        return ox * NY + oy, (z * NX + ox, oy * NC + oc)

    def signal(sem, device):
        pl.semaphore_signal(sem, inc=1, device_id=device, device_id_type=MESH)

    def send(src, dst, send_sem, recv_sem, device):
        pltpu.make_async_remote_copy(
            src_ref=src,
            dst_ref=dst,
            send_sem=send_sem,
            recv_sem=recv_sem,
            device_id=device,
            device_id_type=MESH,
        ).start()

    def wait(ref, sem):
        pltpu.make_async_copy(ref, ref, sem).wait()

    loads = []
    for i, (src, dst) in enumerate(
        (
            (k_hbm, raw.at[0]),
            (v_hbm, raw.at[1]),
            (q_hbm, raw.at[2]),
            (t_hbm, raw.at[3]),
            (kmap_hbm, maps.at[0]),
            (qmap_hbm, maps.at[1]),
        )
    ):
        load = pltpu.make_async_copy(src, dst, load_sem.at[i])
        load.start()
        loads.append(load)

    barrier = pltpu.get_barrier_semaphore()
    near = [at_x(d)[1] for d in X_FAR_FIRST]
    near += [at_z(d)[1] for d in (2, NZ - 2, 1, NZ - 1)]
    near += [at_plane((0, d, 0))[1] for d in (2, 1, 3)]
    near += [at_plane((0, 0, 1))[1]]
    for device in near:
        signal(barrier, device)

    def widen(i):
        wide[i] = raw[i].astype(F32)
        for b in range(2):
            for h in range(2):
                stage[i, b * 2 + h] = wide[i, pl.ds(b * 2 * TOK + h, TOK, stride=2), :]
        held[i, x] = stage[i, x]

    def send_x(i):
        for d in X_FAR_FIRST:
            other, device = at_x(d)
            send(stage.at[i, other], held.at[i, x], x_send.at[i], x_recv.at[i], device)

    loads[0].wait()
    widen(0)
    loads[1].wait()
    widen(1)
    pl.semaphore_wait(barrier, len(near))
    send_x(0)
    send_x(1)
    for d in (2, NZ - 2):
        signal(near_sem, at_z(d)[1])
    for d in (2, 1, 3):
        signal(row_sem, at_plane((0, d, 0))[1])
    loads[2].wait()
    widen(2)
    send_x(2)
    loads[3].wait()
    widen(3)
    send_x(3)
    loads[4].wait()
    loads[5].wait()
    pl.semaphore_wait(near_sem, 2)
    for d in (4, NZ - 4):
        signal(far_sem, at_z(d)[1])
    pl.semaphore_wait(row_sem, 3)
    signal(plane_sem, at_plane((0, 0, 1))[1])

    def receive_x(i):
        wait(held.at[i, pl.ds(0, NX - 1)], x_recv.at[i])
        return held[i].reshape(LOC, DH)

    def scatter_z(scan, full_state, full_norm):
        state[scan, :, :FC, :] = full_state.reshape(NZ, FC, DH)
        for i in range(2):
            state[scan, :, FC + i, :] = jnp.broadcast_to(full_norm[:, i * DH : (i + 1) * DH], (NZ, DH))
        for d in Z_FAR_FIRST:
            other, device = at_z(d)
            send(state.at[scan, other], got_state.at[scan, z], z_send.at[2 * scan], z_recv.at[2 * scan], device)
        got_state[scan, z] = state[scan, z]

    def return_z(scan, reverse):
        wait(got_state.at[scan, pl.ds(0, NZ - 1)], z_recv.at[2 * scan])
        order = range(NZ - 1, -1, -1) if reverse else range(NZ)
        running = jnp.zeros((FC, DH), F32)
        for one in order:
            totals[scan, one] = running
            running = running + got_state[scan, one, :FC, :]
        for d in Z_FAR_FIRST:
            other, device = at_z(d)
            send(totals.at[scan, other], entering.at[scan, z], z_send.at[2 * scan + 1], z_recv.at[2 * scan + 1], device)
        entering[scan, z] = totals[scan, z]
        norm = [jnp.zeros((1, DH), F32)] * 2
        for one in order:
            before = one > z if reverse else one < z
            for i in range(2):
                norm[i] = norm[i] + jnp.where(before, got_state[scan, one, FC + i : FC + i + 1, :], 0.0)
        return jnp.concatenate(norm, 1)

    def receive_z(scan):
        wait(entering.at[scan, pl.ds(0, NZ - 1)], z_recv.at[2 * scan + 1])
        return entering[scan].reshape(F2, DH)

    mine = x * NY + y

    def reduce_plane(which, grad):
        part[which] = grad.reshape(NP, 8, DH)
        for d in PLANE_FAR_FIRST:
            other, device = at_plane(d)
            send(part.at[which, other], got_part.at[which, mine * NC + core], r_send.at[which], r_recv.at[which], device)
        got_part[which, mine * NC + core] = part[which, mine]

    def reduce_z(which):
        wait(got_part.at[which, pl.ds(0, NP * NC - 1)], r_recv.at[which])
        sums[which, 0] = jnp.sum(got_part[which], 0)
        for d in Z_FAR_FIRST:
            send(sums.at[which, 0], got_sum.at[which, z], s_send.at[which], s_recv.at[which], at_z(d)[1])
        got_sum[which, z] = sums[which, 0]

    def share(which):
        wait(got_sum.at[which, pl.ds(0, NZ - 1)], s_recv.at[which])
        sums[which, 1] = jnp.sum(got_sum[which], 0)
        for d in PLANE_FAR_FIRST:
            if not d[2]:
                send(sums.at[which, 1], out_ref.at[which, mine], g_send.at[which], g_recv.at[which], at_plane(d)[1])
        pltpu.make_async_copy(sums.at[which, 1], out_ref.at[which, mine], own_sem.at[which]).start()

    keys = receive_x(0).astype(BF16)
    key_phi = feature(keys, maps[0])
    kphi = split(key_phi)
    key_sum = jnp.sum(key_phi, 0, keepdims=True)
    values = receive_x(1).astype(BF16)
    local = mm2(kphi, values, TN)
    pl.semaphore_wait(far_sem, 2)
    scatter_z(0, local, key_sum)

    queries = receive_x(2).astype(BF16)
    query_phi = feature(queries, maps[1])
    qphi = split(query_phi)

    prefix_norm = return_z(0, False)
    causal = lax.broadcasted_iota(jnp.int32, (LOC, LOC), 0) >= lax.broadcasted_iota(
        jnp.int32, (LOC, LOC), 1
    )
    scores = jnp.where(causal, mm3(qphi, kphi, NT), 0.0)
    inner_num = mm2(split(scores), values, NN)
    denominator = jnp.sum(scores, 1, keepdims=True) + jnp.sum(query_phi * prefix_norm, 1, keepdims=True)
    target = receive_x(3)

    prefix = split(receive_z(0))
    output = (inner_num + mm3(qphi, prefix, NN)) / denominator
    misfit = output - target
    grad_num = misfit / denominator
    grad_den = -jnp.sum(misfit * output, 1, keepdims=True) / denominator
    gnum = split(grad_num)
    scatter_z(1, mm3(qphi, gnum, TN), jnp.sum(query_phi * grad_den, 0, keepdims=True))

    mixed = split(jnp.where(causal, mm2(gnum, values, NT) + grad_den, 0.0))
    query_dphi = mm3(mixed, kphi, NN) + mm3(gnum, prefix, NT) + grad_den * prefix_norm
    grad_aq = split(feature_back(query_phi, query_dphi))
    grad_q = mm(queries, grad_aq[0], TN) + mm(queries, grad_aq[1], TN)
    pl.semaphore_wait(plane_sem, 1)
    reduce_plane(0, grad_q)
    key_inner = mm3(mixed, qphi, TN)

    suffix_norm = return_z(1, True)
    reduce_z(0)
    suffix = split(receive_z(1))
    key_dphi = key_inner + mm(values, suffix[0], NT) + mm(values, suffix[1], NT) + suffix_norm
    grad_ak = split(feature_back(key_phi, key_dphi))
    reduce_plane(1, mm(keys, grad_ak[0], TN) + mm(keys, grad_ak[1], TN))
    share(0)
    reduce_z(1)
    share(1)

    for i in range(4):
        wait(held.at[i, pl.ds(0, NX - 1)], x_send.at[i])
    for scan in range(2):
        wait(state.at[scan, pl.ds(0, NZ - 1)], z_send.at[2 * scan])
        wait(totals.at[scan, pl.ds(0, NZ - 1)], z_send.at[2 * scan + 1])
    for which in range(2):
        wait(got_part.at[which, pl.ds(0, NP * NC - 1)], r_send.at[which])
        wait(got_sum.at[which, pl.ds(0, NZ - 1)], s_send.at[which])
        wait(got_part.at[which, pl.ds(0, NP - 1)], g_send.at[which])
        wait(sums.at[which, 1], own_sem.at[which])
        wait(out_ref.at[which, pl.ds(0, NP - 1)], g_recv.at[which])


def per_device(queries, keys, values, teacher, query_map, key_map):
    def flat(a):
        return a.reshape(-1, DH)

    def dma(*shape):
        return pltpu.SemaphoreType.DMA(shape)

    out = pl.pallas_call(
        kernel,
        out_shape=jax.ShapeDtypeStruct((2, NP, 8, DH), F32),
        in_specs=[pl.BlockSpec(memory_space=pl.ANY)] * 6,
        out_specs=pl.BlockSpec(memory_space=pl.ANY),
        scratch_shapes=[
            pltpu.VMEM((4, 4 * TOK, DH), BF16),
            pltpu.VMEM((2, DH, DH), BF16),
            pltpu.VMEM((4, 4 * TOK, DH), F32),
            pltpu.VMEM((4, 4, TOK, DH), F32),
            pltpu.VMEM((4, NX, TOK, DH), F32),
            pltpu.VMEM((2, NZ, ROWS, DH), F32),
            pltpu.VMEM((2, NZ, ROWS, DH), F32),
            pltpu.VMEM((2, NZ, FC, DH), F32),
            pltpu.VMEM((2, NZ, FC, DH), F32),
            pltpu.VMEM((2, NP, 8, DH), F32),
            pltpu.VMEM((2, NP * NC, 8, DH), F32),
            pltpu.VMEM((2, 2, 8, DH), F32),
            pltpu.VMEM((2, NZ, 8, DH), F32),
            dma(6),
            dma(4),
            dma(4),
            dma(4),
            dma(4),
            dma(2),
            dma(2),
            dma(2),
            dma(2),
            dma(2),
            dma(2),
            dma(2),
            pltpu.SemaphoreType.REGULAR,
            pltpu.SemaphoreType.REGULAR,
            pltpu.SemaphoreType.REGULAR,
            pltpu.SemaphoreType.REGULAR,
        ],
        compiler_params=pltpu.CompilerParams(
            collective_id=0, has_side_effects=True, vmem_limit_bytes=56 * 1024 * 1024
        ),
        name="hedgehog",
    )(flat(keys), flat(values), flat(queries), flat(teacher), query_map, key_map)
    return out[0].reshape(DH, DH), out[1].reshape(DH, DH)


def solution(mesh):
    split_spec = P(None, "seq", "head", None)
    return jax.shard_map(
        per_device,
        mesh=mesh,
        in_specs=(split_spec,) * 4 + (P(), P()),
        out_specs=(P(), P()),
        check_vma=False,
    )
```

time: 87.3 us -> 78.8 us (0.903)
  Pallas kernels: 84.9 us -> 76.1 us
    pallas_call x1, Pallas kernels: 84.9 us -> 76.1 us  [per_device(): pl.pallas_call(kernel, out_shape=jax.ShapeDtypeStruct((2, NP, 8, DH), F32...]
where the time goes in v2:
time: 78.8 us; the launch traced here: 78.2 us
  Pallas kernels  76.1 us (97%)
  local copies, waits for them, and re-layouts  1.53 us (2%)
    pallas_call x1, Pallas kernels, per_device(): pl.pallas_call(kernel, out_shape=jax.ShapeDtypeStruct((2, NP, 8, DH), F32...  76.1 us

profile of v2, /device:TPU:1, one launch (start us, length us, event | category | flops | bytes accessed | tf_op | source)
XLA Modules:
  0.0 78.2 jit_solution(5390394883247112436)
XLA Ops:
  0.6 76.1 %hedgehog.1 = f32[2,16,8,128]{3,2,1,0:T(8,128)} custom-call(bf16[512,128]{1,0:T(8,128)(2,1)} %bitcast.8, bf16[512,128]{1,0:T(8,128)(2,1)} %bitcast.9, bf16[512,128]{1,0:T(8,128)(2,1)} %bitcast.10, bf16[512,128]{1,0:T(8,128)(2,1)} %bitcast.11, bf16[128,128]{1,0:T(8,128)(2,1)} %qmap_hbm.1, bf16[128,128]{1,0:T(8,128)(2,1)} %kmap_hbm.1), custom_call_target="tpu_custom_call" | custom-call | tf_op jit(solution)/shard_map/hedgehog/pallas_call | solution.py:330
  76.7 1.5 %slice_bitcast_fusion = (f32[128,128]{1,0:T(8,128)}, f32[128,128]{1,0:T(8,128)}) fusion(f32[2,16,8,128]{3,2,1,0:T(8,128)} %hedgehog.1), kind=kLoop, calls=%fused_computation | loop fusion | bytes 262144 | tf_op jit(solution)/shard_map/reshape;squeeze | solution.py:371

commit v3 on v2

--- a/solution.py
+++ b/solution.py
@@ -188,10 +188,8 @@
         signal(row_sem, at_plane((0, d, 0))[1])
     loads[2].wait()
     widen(2)
-    send_x(2)
     loads[3].wait()
     widen(3)
-    send_x(3)
     loads[4].wait()
     loads[5].wait()
     pl.semaphore_wait(near_sem, 2)
@@ -267,6 +265,8 @@
     local = mm2(kphi, values, TN)
     pl.semaphore_wait(far_sem, 2)
     scatter_z(0, local, key_sum)
+    send_x(2)
+    send_x(3)
 
     queries = receive_x(2).astype(BF16)
     query_phi = feature(queries, maps[1])

time: 78.8 us -> 77.3 us (0.981)
  Pallas kernels: 76.1 us -> 74.5 us
    pallas_call x1, Pallas kernels: 76.1 us -> 74.5 us  [per_device(): pl.pallas_call(kernel, out_shape=jax.ShapeDtypeStruct((2, NP, 8, DH), F32...]
where the time goes in v3:
time: 77.3 us; the launch traced here: 76.7 us
  Pallas kernels  74.5 us (96%)
  local copies, waits for them, and re-layouts  1.53 us (2%)
    pallas_call x1, Pallas kernels, per_device(): pl.pallas_call(kernel, out_shape=jax.ShapeDtypeStruct((2, NP, 8, DH), F32...  74.5 us

profile of v3, /device:TPU:1, one launch (start us, length us, event | category | flops | bytes accessed | tf_op | source)
XLA Modules:
  0.0 76.7 jit_solution(156949629533711327)
XLA Ops:
  0.6 74.5 %hedgehog.1 = f32[2,16,8,128]{3,2,1,0:T(8,128)} custom-call(bf16[512,128]{1,0:T(8,128)(2,1)} %bitcast.8, bf16[512,128]{1,0:T(8,128)(2,1)} %bitcast.9, bf16[512,128]{1,0:T(8,128)(2,1)} %bitcast.10, bf16[512,128]{1,0:T(8,128)(2,1)} %bitcast.11, bf16[128,128]{1,0:T(8,128)(2,1)} %qmap_hbm.1, bf16[128,128]{1,0:T(8,128)(2,1)} %kmap_hbm.1), custom_call_target="tpu_custom_call" | custom-call | tf_op jit(solution)/shard_map/hedgehog/pallas_call | solution.py:330
  75.2 1.5 %slice_bitcast_fusion = (f32[128,128]{1,0:T(8,128)}, f32[128,128]{1,0:T(8,128)}) fusion(f32[2,16,8,128]{3,2,1,0:T(8,128)} %hedgehog.1), kind=kLoop, calls=%fused_computation | loop fusion | bytes 262144 | tf_op jit(solution)/shard_map/reshape;squeeze | solution.py:371

commit v4 on v3

--- a/solution.py
+++ b/solution.py
@@ -14,7 +14,7 @@
 DH = 128
 F2 = 256
 LOC = NX * TOK
-FC = F2 // NZ
+FC = DH // NZ
 Z_FAR_FIRST = (8, 7, 9, 6, 10, 5, 11, 4, 12, 3, 13, 2, 14, 1, 15)
 X_FAR_FIRST = (2, 1, 3)
 PLANE_FAR_FIRST = tuple(
@@ -24,7 +24,7 @@
     )
 )
 NP = NX * NY
-ROWS = FC + 2
+ROWS = FC + 1
 
 NN = (((1,), (0,)), ((), ()))
 NT = (((1,), (1,)), ((), ()))
@@ -62,12 +62,7 @@
 
 
 def feature_back(phi, dphi):
-    half = phi.shape[-1] // 2
-    up, down = phi[:, :half], phi[:, half:]
-    grad_up, grad_down = dphi[:, :half], dphi[:, half:]
-    return up * (grad_up - jnp.sum(up * grad_up, -1, keepdims=True)) - down * (
-        grad_down - jnp.sum(down * grad_down, -1, keepdims=True)
-    )
+    return phi * (dphi - jnp.sum(phi * dphi, -1, keepdims=True))
 
 
 def kernel(
@@ -202,36 +197,38 @@
         wait(held.at[i, pl.ds(0, NX - 1)], x_recv.at[i])
         return held[i].reshape(LOC, DH)
 
-    def scatter_z(scan, full_state, full_norm):
-        state[scan, :, :FC, :] = full_state.reshape(NZ, FC, DH)
-        for i in range(2):
-            state[scan, :, FC + i, :] = jnp.broadcast_to(full_norm[:, i * DH : (i + 1) * DH], (NZ, DH))
+    def scatter_z(scan, sign, rows, norm):
+        state[scan, sign, :, :FC, :] = rows.reshape(NZ, FC, DH)
+        state[scan, sign, :, FC, :] = jnp.broadcast_to(norm, (NZ, DH))
+        sem = 4 * scan + sign
         for d in Z_FAR_FIRST:
             other, device = at_z(d)
-            send(state.at[scan, other], got_state.at[scan, z], z_send.at[2 * scan], z_recv.at[2 * scan], device)
-        got_state[scan, z] = state[scan, z]
-
-    def return_z(scan, reverse):
-        wait(got_state.at[scan, pl.ds(0, NZ - 1)], z_recv.at[2 * scan])
+            send(state.at[scan, sign, other], got_state.at[scan, sign, z], z_send.at[sem], z_recv.at[sem], device)
+        got_state[scan, sign, z] = state[scan, sign, z]
+
+    def return_z(scan, sign, reverse):
+        sem = 4 * scan + sign
+        wait(got_state.at[scan, sign, pl.ds(0, NZ - 1)], z_recv.at[sem])
         order = range(NZ - 1, -1, -1) if reverse else range(NZ)
         running = jnp.zeros((FC, DH), F32)
         for one in order:
-            totals[scan, one] = running
-            running = running + got_state[scan, one, :FC, :]
+            totals[scan, sign, one] = running
+            running = running + got_state[scan, sign, one, :FC, :]
         for d in Z_FAR_FIRST:
             other, device = at_z(d)
-            send(totals.at[scan, other], entering.at[scan, z], z_send.at[2 * scan + 1], z_recv.at[2 * scan + 1], device)
-        entering[scan, z] = totals[scan, z]
-        norm = [jnp.zeros((1, DH), F32)] * 2
-        for one in order:
+            send(totals.at[scan, sign, other], entering.at[scan, sign, z], z_send.at[sem + 2], z_recv.at[sem + 2], device)
+        entering[scan, sign, z] = totals[scan, sign, z]
+
+    def norm_z(scan, sign, reverse):
+        norm = jnp.zeros((1, DH), F32)
+        for one in range(NZ):
             before = one > z if reverse else one < z
-            for i in range(2):
-                norm[i] = norm[i] + jnp.where(before, got_state[scan, one, FC + i : FC + i + 1, :], 0.0)
-        return jnp.concatenate(norm, 1)
-
-    def receive_z(scan):
-        wait(entering.at[scan, pl.ds(0, NZ - 1)], z_recv.at[2 * scan + 1])
-        return entering[scan].reshape(F2, DH)
+            norm = norm + jnp.where(before, got_state[scan, sign, one, FC : FC + 1, :], 0.0)
+        return norm
+
+    def receive_z(scan, sign):
+        wait(entering.at[scan, sign, pl.ds(0, NZ - 1)], z_recv.at[4 * scan + sign + 2])
+        return entering[scan, sign].reshape(DH, DH)
 
     mine = x * NY + y
 
@@ -257,14 +254,19 @@
                 send(sums.at[which, 1], out_ref.at[which, mine], g_send.at[which], g_recv.at[which], at_plane(d)[1])
         pltpu.make_async_copy(sums.at[which, 1], out_ref.at[which, mine], own_sem.at[which]).start()
 
+    def of(sign, pair):
+        return tuple(a[:, sign * DH : (sign + 1) * DH] for a in pair)
+
     keys = receive_x(0).astype(BF16)
     key_phi = feature(keys, maps[0])
     kphi = split(key_phi)
     key_sum = jnp.sum(key_phi, 0, keepdims=True)
     values = receive_x(1).astype(BF16)
-    local = mm2(kphi, values, TN)
-    pl.semaphore_wait(far_sem, 2)
-    scatter_z(0, local, key_sum)
+    for sign in range(2):
+        local = mm2(of(sign, kphi), values, TN)
+        if sign == 0:
+            pl.semaphore_wait(far_sem, 2)
+        scatter_z(0, sign, local, key_sum[:, sign * DH : (sign + 1) * DH])
     send_x(2)
     send_x(3)
 
@@ -272,36 +274,56 @@
     query_phi = feature(queries, maps[1])
     qphi = split(query_phi)
 
-    prefix_norm = return_z(0, False)
+    for sign in range(2):
+        return_z(0, sign, False)
+    prefix_norm = jnp.concatenate([norm_z(0, sign, False) for sign in range(2)], 1)
     causal = lax.broadcasted_iota(jnp.int32, (LOC, LOC), 0) >= lax.broadcasted_iota(
         jnp.int32, (LOC, LOC), 1
     )
     scores = jnp.where(causal, mm3(qphi, kphi, NT), 0.0)
-    inner_num = mm2(split(scores), values, NN)
+    numerator = mm2(split(scores), values, NN)
     denominator = jnp.sum(scores, 1, keepdims=True) + jnp.sum(query_phi * prefix_norm, 1, keepdims=True)
     target = receive_x(3)
 
-    prefix = split(receive_z(0))
-    output = (inner_num + mm3(qphi, prefix, NN)) / denominator
+    prefix = []
+    for sign in range(2):
+        prefix.append(split(receive_z(0, sign)))
+        numerator = numerator + mm3(of(sign, qphi), prefix[sign], NN)
+    output = numerator / denominator
     misfit = output - target
     grad_num = misfit / denominator
     grad_den = -jnp.sum(misfit * output, 1, keepdims=True) / denominator
     gnum = split(grad_num)
-    scatter_z(1, mm3(qphi, gnum, TN), jnp.sum(query_phi * grad_den, 0, keepdims=True))
+    query_sum = jnp.sum(query_phi * grad_den, 0, keepdims=True)
+    for sign in range(2):
+        scatter_z(1, sign, mm3(of(sign, qphi), gnum, TN), query_sum[:, sign * DH : (sign + 1) * DH])
 
     mixed = split(jnp.where(causal, mm2(gnum, values, NT) + grad_den, 0.0))
-    query_dphi = mm3(mixed, kphi, NN) + mm3(gnum, prefix, NT) + grad_den * prefix_norm
-    grad_aq = split(feature_back(query_phi, query_dphi))
+    query_dphi = (
+        mm3(mixed, kphi, NN)
+        + jnp.concatenate([mm3(gnum, prefix[sign], NT) for sign in range(2)], 1)
+        + grad_den * prefix_norm
+    )
+    grad_aq = split(
+        feature_back(query_phi[:, :DH], query_dphi[:, :DH]) - feature_back(query_phi[:, DH:], query_dphi[:, DH:])
+    )
     grad_q = mm(queries, grad_aq[0], TN) + mm(queries, grad_aq[1], TN)
     pl.semaphore_wait(plane_sem, 1)
     reduce_plane(0, grad_q)
     key_inner = mm3(mixed, qphi, TN)
 
-    suffix_norm = return_z(1, True)
+    for sign in range(2):
+        return_z(1, sign, True)
+    suffix_norm = jnp.concatenate([norm_z(1, sign, True) for sign in range(2)], 1)
+    key_inner = key_inner + suffix_norm
     reduce_z(0)
-    suffix = split(receive_z(1))
-    key_dphi = key_inner + mm(values, suffix[0], NT) + mm(values, suffix[1], NT) + suffix_norm
-    grad_ak = split(feature_back(key_phi, key_dphi))
+    grad_ak = []
+    for sign in range(2):
+        suffix = split(receive_z(1, sign))
+        lanes = slice(sign * DH, (sign + 1) * DH)
+        key_dphi = key_inner[:, lanes] + mm(values, suffix[0], NT) + mm(values, suffix[1], NT)
+        grad_ak.append(feature_back(key_phi[:, lanes], key_dphi))
+    grad_ak = split(grad_ak[0] - grad_ak[1])
     reduce_plane(1, mm(keys, grad_ak[0], TN) + mm(keys, grad_ak[1], TN))
     share(0)
     reduce_z(1)
@@ -310,8 +332,9 @@
     for i in range(4):
         wait(held.at[i, pl.ds(0, NX - 1)], x_send.at[i])
     for scan in range(2):
-        wait(state.at[scan, pl.ds(0, NZ - 1)], z_send.at[2 * scan])
-        wait(totals.at[scan, pl.ds(0, NZ - 1)], z_send.at[2 * scan + 1])
+        for sign in range(2):
+            wait(state.at[scan, sign, pl.ds(0, NZ - 1)], z_send.at[4 * scan + sign])
+            wait(totals.at[scan, sign, pl.ds(0, NZ - 1)], z_send.at[4 * scan + sign + 2])
     for which in range(2):
         wait(got_part.at[which, pl.ds(0, NP * NC - 1)], r_send.at[which])
         wait(got_sum.at[which, pl.ds(0, NZ - 1)], s_send.at[which])
@@ -338,10 +361,10 @@
             pltpu.VMEM((4, 4 * TOK, DH), F32),
             pltpu.VMEM((4, 4, TOK, DH), F32),
             pltpu.VMEM((4, NX, TOK, DH), F32),
-            pltpu.VMEM((2, NZ, ROWS, DH), F32),
-            pltpu.VMEM((2, NZ, ROWS, DH), F32),
-            pltpu.VMEM((2, NZ, FC, DH), F32),
-            pltpu.VMEM((2, NZ, FC, DH), F32),
+            pltpu.VMEM((2, 2, NZ, ROWS, DH), F32),
+            pltpu.VMEM((2, 2, NZ, ROWS, DH), F32),
+            pltpu.VMEM((2, 2, NZ, FC, DH), F32),
+            pltpu.VMEM((2, 2, NZ, FC, DH), F32),
             pltpu.VMEM((2, NP, 8, DH), F32),
             pltpu.VMEM((2, NP * NC, 8, DH), F32),
             pltpu.VMEM((2, 2, 8, DH), F32),
@@ -349,8 +372,8 @@
             dma(6),
             dma(4),
             dma(4),
-            dma(4),
-            dma(4),
+            dma(8),
+            dma(8),
             dma(2),
             dma(2),
             dma(2),

time: 77.3 us -> 75.1 us (0.972)
  Pallas kernels: 74.5 us -> 72.5 us
    pallas_call x1, Pallas kernels: 74.5 us -> 72.5 us  [per_device(): pl.pallas_call(kernel, out_shape=jax.ShapeDtypeStruct((2, NP, 8, DH), F32...]
where the time goes in v4:
time: 75.1 us; the launch traced here: 74.7 us
  Pallas kernels  72.5 us (97%)
  local copies, waits for them, and re-layouts  1.53 us (2%)
    pallas_call x1, Pallas kernels, per_device(): pl.pallas_call(kernel, out_shape=jax.ShapeDtypeStruct((2, NP, 8, DH), F32...  72.5 us
    another operation x1, local copies, waits for them, and re-layouts, per_device(): return (out[0].reshape(DH, DH), out[1].reshape(DH, DH))  1.53 us

profile of v4, /device:TPU:1, one launch (start us, length us, event | category | flops | bytes accessed | tf_op | source)
XLA Modules:
  0.0 74.7 jit_solution(11791142566544405749)
XLA Ops:
  0.6 72.5 %hedgehog.1 = f32[2,16,8,128]{3,2,1,0:T(8,128)} custom-call(bf16[512,128]{1,0:T(8,128)(2,1)} %bitcast.8, bf16[512,128]{1,0:T(8,128)(2,1)} %bitcast.9, bf16[512,128]{1,0:T(8,128)(2,1)} %bitcast.10, bf16[512,128]{1,0:T(8,128)(2,1)} %bitcast.11, bf16[128,128]{1,0:T(8,128)(2,1)} %qmap_hbm.1, bf16[128,128]{1,0:T(8,128)(2,1)} %kmap_hbm.1), custom_call_target="tpu_custom_call" | custom-call | tf_op jit(solution)/shard_map/hedgehog/pallas_call | solution.py:353
  73.2 1.5 %slice_bitcast_fusion = (f32[128,128]{1,0:T(8,128)}, f32[128,128]{1,0:T(8,128)}) fusion(f32[2,16,8,128]{3,2,1,0:T(8,128)} %hedgehog.1), kind=kLoop, calls=%fused_computation | loop fusion | bytes 262144 | tf_op jit(solution)/shard_map/reshape;squeeze | solution.py:394

commit v5 on v4

--- a/solution.py
+++ b/solution.py
@@ -15,7 +15,9 @@
 F2 = 256
 LOC = NX * TOK
 FC = DH // NZ
-Z_FAR_FIRST = (8, 7, 9, 6, 10, 5, 11, 4, 12, 3, 13, 2, 14, 1, 15)
+Z_FAR = (8, 7, 9, 6, 10, 5, 11)
+Z_NEAR = (4, 12, 3, 13, 2, 14, 1, 15)
+Z_FAR_FIRST = Z_FAR + Z_NEAR
 X_FAR_FIRST = (2, 1, 3)
 PLANE_FAR_FIRST = tuple(
     sorted(
@@ -24,7 +26,7 @@
     )
 )
 NP = NX * NY
-ROWS = FC + 1
+HALF = DH // 2
 
 NN = (((1,), (0,)), ((), ()))
 NT = (((1,), (1,)), ((), ()))
@@ -46,6 +48,15 @@
 
 def mm2(a, b, dims):
     return mm(a[0], b, dims) + mm(a[1], b, dims)
+
+
+def mm_wide(a, b):
+    both = mm(a, b, NN)
+    return both[:, :DH] + both[:, DH:]
+
+
+def side(pair):
+    return jnp.concatenate(pair, 1)
 
 
 def feature(inputs, matrix):
@@ -78,8 +89,14 @@
     wide,
     stage,
     held,
-    state,
-    got_state,
+    stage_v,
+    held_v,
+    state_a,
+    got_state_a,
+    state_b,
+    got_state_b,
+    state_c,
+    got_state_c,
     totals,
     entering,
     part,
@@ -135,6 +152,14 @@
     def wait(ref, sem):
         pltpu.make_async_copy(ref, ref, sem).wait()
 
+    barrier = pltpu.get_barrier_semaphore()
+    near = [at_x(d)[1] for d in X_FAR_FIRST]
+    near += [at_z(d)[1] for d in (2, NZ - 2, 1, NZ - 1)]
+    near += [at_plane((0, d, 0))[1] for d in (2, 1, 3)]
+    near += [at_plane((0, 0, 1))[1]]
+    for device in near:
+        signal(barrier, device)
+
     loads = []
     for i, (src, dst) in enumerate(
         (
@@ -150,41 +175,49 @@
         load.start()
         loads.append(load)
 
-    barrier = pltpu.get_barrier_semaphore()
-    near = [at_x(d)[1] for d in X_FAR_FIRST]
-    near += [at_z(d)[1] for d in (2, NZ - 2, 1, NZ - 1)]
-    near += [at_plane((0, d, 0))[1] for d in (2, 1, 3)]
-    near += [at_plane((0, 0, 1))[1]]
-    for device in near:
-        signal(barrier, device)
-
-    def widen(i):
-        wide[i] = raw[i].astype(F32)
+    def widen(i, source):
+        wide[source] = raw[source].astype(F32)
         for b in range(2):
             for h in range(2):
-                stage[i, b * 2 + h] = wide[i, pl.ds(b * 2 * TOK + h, TOK, stride=2), :]
+                stage[i, b * 2 + h] = wide[source, pl.ds(b * 2 * TOK + h, TOK, stride=2), :]
         held[i, x] = stage[i, x]
+
+    def widen_v():
+        wide[1] = raw[1].astype(F32)
+        for b in range(2):
+            for h in range(2):
+                turned = wide[1, pl.ds(b * 2 * TOK + h, TOK, stride=2), :].T
+                for half in range(2):
+                    stage_v[half, b * 2 + h] = turned[half * HALF : (half + 1) * HALF]
+        for half in range(2):
+            held_v[half, x] = stage_v[half, x]
 
     def send_x(i):
         for d in X_FAR_FIRST:
             other, device = at_x(d)
             send(stage.at[i, other], held.at[i, x], x_send.at[i], x_recv.at[i], device)
 
+    def send_v(half):
+        for d in X_FAR_FIRST:
+            other, device = at_x(d)
+            send(stage_v.at[half, other], held_v.at[half, x], x_send.at[3 + half], x_recv.at[3 + half], device)
+
     loads[0].wait()
-    widen(0)
+    widen(0, 0)
     loads[1].wait()
-    widen(1)
+    widen_v()
     pl.semaphore_wait(barrier, len(near))
     send_x(0)
-    send_x(1)
+    send_v(0)
+    send_v(1)
     for d in (2, NZ - 2):
         signal(near_sem, at_z(d)[1])
     for d in (2, 1, 3):
         signal(row_sem, at_plane((0, d, 0))[1])
     loads[2].wait()
-    widen(2)
+    widen(1, 2)
     loads[3].wait()
-    widen(3)
+    widen(2, 3)
     loads[4].wait()
     loads[5].wait()
     pl.semaphore_wait(near_sem, 2)
@@ -197,42 +230,61 @@
         wait(held.at[i, pl.ds(0, NX - 1)], x_recv.at[i])
         return held[i].reshape(LOC, DH)
 
-    def scatter_z(scan, sign, rows, norm):
-        state[scan, sign, :, :FC, :] = rows.reshape(NZ, FC, DH)
-        state[scan, sign, :, FC, :] = jnp.broadcast_to(norm, (NZ, DH))
-        sem = 4 * scan + sign
-        for d in Z_FAR_FIRST:
+    def receive_v(half):
+        wait(held_v.at[half, pl.ds(0, NX - 1)], x_recv.at[3 + half])
+        return jnp.concatenate([held_v[half, i] for i in range(NX)], 1).astype(BF16)
+
+    streams = (
+        ((state_a, got_state_a), (state_b, got_state_b)),
+        tuple((state_c.at[sign], got_state_c.at[sign]) for sign in range(2)),
+    )
+
+    def scatter_z(scan, stream):
+        rows, got = streams[scan][stream]
+        got[z] = rows[z]
+        send_rows(scan, stream, Z_FAR)
+
+    def send_rows(scan, stream, distances):
+        rows, got = streams[scan][stream]
+        sem = 4 * scan + stream
+        for d in distances:
             other, device = at_z(d)
-            send(state.at[scan, sign, other], got_state.at[scan, sign, z], z_send.at[sem], z_recv.at[sem], device)
-        got_state[scan, sign, z] = state[scan, sign, z]
-
-    def return_z(scan, sign, reverse):
-        sem = 4 * scan + sign
-        wait(got_state.at[scan, sign, pl.ds(0, NZ - 1)], z_recv.at[sem])
+            send(rows.at[other], got.at[z], z_send.at[sem], z_recv.at[sem], device)
+
+    def return_z(scan, stream, reverse):
+        got = streams[scan][stream][1]
+        sem = 4 * scan + stream
+        wait(got.at[pl.ds(0, NZ - 1)], z_recv.at[sem])
         order = range(NZ - 1, -1, -1) if reverse else range(NZ)
         running = jnp.zeros((FC, DH), F32)
         for one in order:
-            totals[scan, sign, one] = running
-            running = running + got_state[scan, sign, one, :FC, :]
-        for d in Z_FAR_FIRST:
+            totals[scan, stream, one] = running
+            running = running + got[one, :FC, :]
+        entering[scan, stream, z] = totals[scan, stream, z]
+        send_totals(scan, stream, Z_FAR)
+
+    def send_totals(scan, stream, distances):
+        sem = 4 * scan + stream + 2
+        for d in distances:
             other, device = at_z(d)
-            send(totals.at[scan, sign, other], entering.at[scan, sign, z], z_send.at[sem + 2], z_recv.at[sem + 2], device)
-        entering[scan, sign, z] = totals[scan, sign, z]
-
-    def norm_z(scan, sign, reverse):
+            send(totals.at[scan, stream, other], entering.at[scan, stream, z], z_send.at[sem], z_recv.at[sem], device)
+
+    def norm_z(got, row, reverse):
         norm = jnp.zeros((1, DH), F32)
         for one in range(NZ):
             before = one > z if reverse else one < z
-            norm = norm + jnp.where(before, got_state[scan, sign, one, FC : FC + 1, :], 0.0)
+            norm = norm + jnp.where(before, got[one, row : row + 1, :], 0.0)
         return norm
 
-    def receive_z(scan, sign):
-        wait(entering.at[scan, sign, pl.ds(0, NZ - 1)], z_recv.at[4 * scan + sign + 2])
-        return entering[scan, sign].reshape(DH, DH)
+    def receive_z(scan, stream):
+        wait(entering.at[scan, stream, pl.ds(0, NZ - 1)], z_recv.at[4 * scan + stream + 2])
+        return entering[scan, stream]
 
     mine = x * NY + y
 
     def reduce_plane(which, grad):
+        if which == 0:
+            pl.semaphore_wait(plane_sem, 1)
         part[which] = grad.reshape(NP, 8, DH)
         for d in PLANE_FAR_FIRST:
             other, device = at_plane(d)
@@ -254,87 +306,108 @@
                 send(sums.at[which, 1], out_ref.at[which, mine], g_send.at[which], g_recv.at[which], at_plane(d)[1])
         pltpu.make_async_copy(sums.at[which, 1], out_ref.at[which, mine], own_sem.at[which]).start()
 
-    def of(sign, pair):
-        return tuple(a[:, sign * DH : (sign + 1) * DH] for a in pair)
-
     keys = receive_x(0).astype(BF16)
     key_phi = feature(keys, maps[0])
     kphi = split(key_phi)
     key_sum = jnp.sum(key_phi, 0, keepdims=True)
-    values = receive_x(1).astype(BF16)
-    for sign in range(2):
-        local = mm2(of(sign, kphi), values, TN)
-        if sign == 0:
+    for i in range(2):
+        state_a[:, FC + i, :] = jnp.broadcast_to(key_sum[:, i * DH : (i + 1) * DH], (NZ, DH))
+    values_t = []
+    for half in range(2):
+        values_t.append(receive_v(half))
+        local = mm(values_t[half], kphi[0], NN) + mm(values_t[half], kphi[1], NN)
+        rows = streams[0][half][0]
+        for owner in range(NZ):
+            i, j = owner // 2, owner % 2
+            rows[owner, :FC, :] = local[i * FC : (i + 1) * FC, j * DH : (j + 1) * DH]
+        if half == 0:
             pl.semaphore_wait(far_sem, 2)
-        scatter_z(0, sign, local, key_sum[:, sign * DH : (sign + 1) * DH])
+        scatter_z(0, half)
+    for half in range(2):
+        send_rows(0, half, Z_NEAR)
+    send_x(1)
     send_x(2)
-    send_x(3)
-
-    queries = receive_x(2).astype(BF16)
+    values_t = jnp.concatenate(values_t, 0)
+    values = values_t.T
+
+    queries = receive_x(1).astype(BF16)
     query_phi = feature(queries, maps[1])
     qphi = split(query_phi)
 
-    for sign in range(2):
-        return_z(0, sign, False)
-    prefix_norm = jnp.concatenate([norm_z(0, sign, False) for sign in range(2)], 1)
+    for half in range(2):
+        return_z(0, half, False)
+    for half in range(2):
+        send_totals(0, half, Z_NEAR)
+    prefix_norm = side([norm_z(got_state_a, FC + i, False) for i in range(2)])
     causal = lax.broadcasted_iota(jnp.int32, (LOC, LOC), 0) >= lax.broadcasted_iota(
         jnp.int32, (LOC, LOC), 1
     )
     scores = jnp.where(causal, mm3(qphi, kphi, NT), 0.0)
-    numerator = mm2(split(scores), values, NN)
+    inner_num = mm2(split(scores), values, NN)
     denominator = jnp.sum(scores, 1, keepdims=True) + jnp.sum(query_phi * prefix_norm, 1, keepdims=True)
-    target = receive_x(3)
+    target = receive_x(2)
+    qphi_t = tuple(a.T for a in qphi)
+    keys_t = keys.T
 
     prefix = []
-    for sign in range(2):
-        prefix.append(split(receive_z(0, sign)))
-        numerator = numerator + mm3(of(sign, qphi), prefix[sign], NN)
+    for half in range(2):
+        blocks = receive_z(0, half)
+        for i in range(NZ // 2):
+            prefix.append(side([blocks[2 * i], blocks[2 * i + 1]]))
+    prefix = split(jnp.concatenate(prefix, 0))
+    both = mm(qphi[0], jnp.concatenate(prefix, 0), NT)
+    numerator = inner_num + (both[:, :DH] + (both[:, DH:] + mm(qphi[1], prefix[0], NT)))
     output = numerator / denominator
     misfit = output - target
     grad_num = misfit / denominator
     grad_den = -jnp.sum(misfit * output, 1, keepdims=True) / denominator
     gnum = split(grad_num)
+    gnum_side = side(gnum)
     query_sum = jnp.sum(query_phi * grad_den, 0, keepdims=True)
     for sign in range(2):
-        scatter_z(1, sign, mm3(of(sign, qphi), gnum, TN), query_sum[:, sign * DH : (sign + 1) * DH])
+        lanes = slice(sign * DH, (sign + 1) * DH)
+        back = mm_wide(qphi_t[0][lanes], gnum_side) + mm(qphi_t[1][lanes], gnum[0], NN)
+        state_c[sign, :, :FC, :] = back.reshape(NZ, FC, DH)
+        state_c[sign, :, FC, :] = jnp.broadcast_to(query_sum[:, lanes], (NZ, DH))
+        scatter_z(1, sign)
+    for sign in range(2):
+        send_rows(1, sign, Z_NEAR)
 
     mixed = split(jnp.where(causal, mm2(gnum, values, NT) + grad_den, 0.0))
-    query_dphi = (
-        mm3(mixed, kphi, NN)
-        + jnp.concatenate([mm3(gnum, prefix[sign], NT) for sign in range(2)], 1)
-        + grad_den * prefix_norm
-    )
+    query_dphi = mm3(mixed, kphi, NN) + mm3(gnum, prefix, NN) + grad_den * prefix_norm
     grad_aq = split(
         feature_back(query_phi[:, :DH], query_dphi[:, :DH]) - feature_back(query_phi[:, DH:], query_dphi[:, DH:])
     )
-    grad_q = mm(queries, grad_aq[0], TN) + mm(queries, grad_aq[1], TN)
-    pl.semaphore_wait(plane_sem, 1)
-    reduce_plane(0, grad_q)
+    reduce_plane(0, mm_wide(queries.T, side(grad_aq)))
     key_inner = mm3(mixed, qphi, TN)
 
     for sign in range(2):
         return_z(1, sign, True)
-    suffix_norm = jnp.concatenate([norm_z(1, sign, True) for sign in range(2)], 1)
+    for sign in range(2):
+        send_totals(1, sign, Z_NEAR)
+    suffix_norm = side([norm_z(got_state_c.at[sign], FC, True) for sign in range(2)])
     key_inner = key_inner + suffix_norm
     reduce_z(0)
     grad_ak = []
     for sign in range(2):
-        suffix = split(receive_z(1, sign))
+        suffix = split(receive_z(1, sign).reshape(DH, DH))
         lanes = slice(sign * DH, (sign + 1) * DH)
-        key_dphi = key_inner[:, lanes] + mm(values, suffix[0], NT) + mm(values, suffix[1], NT)
-        grad_ak.append(feature_back(key_phi[:, lanes], key_dphi))
-    grad_ak = split(grad_ak[0] - grad_ak[1])
-    reduce_plane(1, mm(keys, grad_ak[0], TN) + mm(keys, grad_ak[1], TN))
+        both = mm(values, jnp.concatenate(suffix, 0), NT)
+        grad_ak.append(feature_back(key_phi[:, lanes], key_inner[:, lanes] + (both[:, :DH] + both[:, DH:])))
+    reduce_plane(1, mm_wide(keys_t, side(split(grad_ak[0] - grad_ak[1]))))
     share(0)
     reduce_z(1)
     share(1)
 
-    for i in range(4):
+    for i in range(3):
         wait(held.at[i, pl.ds(0, NX - 1)], x_send.at[i])
+    for half in range(2):
+        wait(held_v.at[half, pl.ds(0, NX - 1)], x_send.at[3 + half])
     for scan in range(2):
-        for sign in range(2):
-            wait(state.at[scan, sign, pl.ds(0, NZ - 1)], z_send.at[4 * scan + sign])
-            wait(totals.at[scan, sign, pl.ds(0, NZ - 1)], z_send.at[4 * scan + sign + 2])
+        for stream in range(2):
+            rows = streams[scan][stream][0]
+            wait(rows.at[pl.ds(0, NZ - 1)], z_send.at[4 * scan + stream])
+            wait(totals.at[scan, stream, pl.ds(0, NZ - 1)], z_send.at[4 * scan + stream + 2])
     for which in range(2):
         wait(got_part.at[which, pl.ds(0, NP * NC - 1)], r_send.at[which])
         wait(got_sum.at[which, pl.ds(0, NZ - 1)], s_send.at[which])
@@ -359,10 +432,16 @@
             pltpu.VMEM((4, 4 * TOK, DH), BF16),
             pltpu.VMEM((2, DH, DH), BF16),
             pltpu.VMEM((4, 4 * TOK, DH), F32),
-            pltpu.VMEM((4, 4, TOK, DH), F32),
-            pltpu.VMEM((4, NX, TOK, DH), F32),
-            pltpu.VMEM((2, 2, NZ, ROWS, DH), F32),
-            pltpu.VMEM((2, 2, NZ, ROWS, DH), F32),
+            pltpu.VMEM((3, 4, TOK, DH), F32),
+            pltpu.VMEM((3, NX, TOK, DH), F32),
+            pltpu.VMEM((2, 4, HALF, TOK), F32),
+            pltpu.VMEM((2, NX, HALF, TOK), F32),
+            pltpu.VMEM((NZ, FC + 2, DH), F32),
+            pltpu.VMEM((NZ, FC + 2, DH), F32),
+            pltpu.VMEM((NZ, FC, DH), F32),
+            pltpu.VMEM((NZ, FC, DH), F32),
+            pltpu.VMEM((2, NZ, FC + 1, DH), F32),
+            pltpu.VMEM((2, NZ, FC + 1, DH), F32),
             pltpu.VMEM((2, 2, NZ, FC, DH), F32),
             pltpu.VMEM((2, 2, NZ, FC, DH), F32),
             pltpu.VMEM((2, NP, 8, DH), F32),
@@ -370,8 +449,8 @@
             pltpu.VMEM((2, 2, 8, DH), F32),
             pltpu.VMEM((2, NZ, 8, DH), F32),
             dma(6),
-            dma(4),
-            dma(4),
+            dma(5),
+            dma(5),
             dma(8),
             dma(8),
             dma(2),

time: 75.1 us -> 74.7 us (level)
  Pallas kernels: 72.5 us -> 71.6 us
    pallas_call x1, Pallas kernels: 72.5 us -> 71.6 us  [per_device(): pl.pallas_call(kernel, out_shape=jax.ShapeDtypeStruct((2, NP, 8, DH), F32...]
where the time goes in v5:
time: 74.7 us; the launch traced here: 73.8 us
  Pallas kernels  71.6 us (96%)
  local copies, waits for them, and re-layouts  1.53 us (2%)
    pallas_call x1, Pallas kernels, per_device(): pl.pallas_call(kernel, out_shape=jax.ShapeDtypeStruct((2, NP, 8, DH), F32...  71.6 us
    another operation x1, local copies, waits for them, and re-layouts, per_device(): return (out[0].reshape(DH, DH), out[1].reshape(DH, DH))  1.53 us

profile of v5, /device:TPU:1, one launch (start us, length us, event | category | flops | bytes accessed | tf_op | source)
XLA Modules:
  0.0 73.8 jit_solution(10519690070693279998)
XLA Ops:
  0.6 71.6 %hedgehog.1 = f32[2,16,8,128]{3,2,1,0:T(8,128)} custom-call(bf16[512,128]{1,0:T(8,128)(2,1)} %bitcast.8, bf16[512,128]{1,0:T(8,128)(2,1)} %bitcast.9, bf16[512,128]{1,0:T(8,128)(2,1)} %bitcast.10, bf16[512,128]{1,0:T(8,128)(2,1)} %bitcast.11, bf16[128,128]{1,0:T(8,128)(2,1)} %qmap_hbm.1, bf16[128,128]{1,0:T(8,128)(2,1)} %kmap_hbm.1), custom_call_target="tpu_custom_call" | custom-call | tf_op jit(solution)/shard_map/hedgehog/pallas_call | solution.py:426
  72.2 1.5 %slice_bitcast_fusion = (f32[128,128]{1,0:T(8,128)}, f32[128,128]{1,0:T(8,128)}) fusion(f32[2,16,8,128]{3,2,1,0:T(8,128)} %hedgehog.1), kind=kLoop, calls=%fused_computation | loop fusion | bytes 262144 | tf_op jit(solution)/shard_map/reshape;squeeze | solution.py:473

commit v6 on v5

--- a/solution.py
+++ b/solution.py
@@ -286,7 +286,7 @@
         if which == 0:
             pl.semaphore_wait(plane_sem, 1)
         part[which] = grad.reshape(NP, 8, DH)
-        for d in PLANE_FAR_FIRST:
+        for d in sorted(PLANE_FAR_FIRST, key=lambda d: d[2]):
             other, device = at_plane(d)
             send(part.at[which, other], got_part.at[which, mine * NC + core], r_send.at[which], r_recv.at[which], device)
         got_part[which, mine * NC + core] = part[which, mine]
@@ -330,15 +330,15 @@
     values_t = jnp.concatenate(values_t, 0)
     values = values_t.T
 
+    for half in range(2):
+        return_z(0, half, False)
+    for half in range(2):
+        send_totals(0, half, Z_NEAR)
+    prefix_norm = side([norm_z(got_state_a, FC + i, False) for i in range(2)])
     queries = receive_x(1).astype(BF16)
     query_phi = feature(queries, maps[1])
     qphi = split(query_phi)
 
-    for half in range(2):
-        return_z(0, half, False)
-    for half in range(2):
-        send_totals(0, half, Z_NEAR)
-    prefix_norm = side([norm_z(got_state_a, FC + i, False) for i in range(2)])
     causal = lax.broadcasted_iota(jnp.int32, (LOC, LOC), 0) >= lax.broadcasted_iota(
         jnp.int32, (LOC, LOC), 1
     )
@@ -395,8 +395,8 @@
         both = mm(values, jnp.concatenate(suffix, 0), NT)
         grad_ak.append(feature_back(key_phi[:, lanes], key_inner[:, lanes] + (both[:, :DH] + both[:, DH:])))
     reduce_plane(1, mm_wide(keys_t, side(split(grad_ak[0] - grad_ak[1]))))
+    reduce_z(1)
     share(0)
-    reduce_z(1)
     share(1)
 
     for i in range(3):

time: 74.7 us -> 73.4 us (0.983)
  Pallas kernels: 71.6 us -> 70.4 us
    pallas_call x1, Pallas kernels: 71.6 us -> 70.4 us  [per_device(): pl.pallas_call(kernel, out_shape=jax.ShapeDtypeStruct((2, NP, 8, DH), F32...]
where the time goes in v6:
time: 73.4 us; the launch traced here: 72.6 us
  Pallas kernels  70.4 us (96%)
  local copies, waits for them, and re-layouts  1.53 us (2%)
    pallas_call x1, Pallas kernels, per_device(): pl.pallas_call(kernel, out_shape=jax.ShapeDtypeStruct((2, NP, 8, DH), F32...  70.4 us
    another operation x1, local copies, waits for them, and re-layouts, per_device(): return (out[0].reshape(DH, DH), out[1].reshape(DH, DH))  1.53 us

profile of v6, /device:TPU:1, one launch (start us, length us, event | category | flops | bytes accessed | tf_op | source)
XLA Modules:
  0.0 72.6 jit_solution(225605970418202432)
XLA Ops:
  0.6 70.4 %hedgehog.1 = f32[2,16,8,128]{3,2,1,0:T(8,128)} custom-call(bf16[512,128]{1,0:T(8,128)(2,1)} %bitcast.8, bf16[512,128]{1,0:T(8,128)(2,1)} %bitcast.9, bf16[512,128]{1,0:T(8,128)(2,1)} %bitcast.10, bf16[512,128]{1,0:T(8,128)(2,1)} %bitcast.11, bf16[128,128]{1,0:T(8,128)(2,1)} %qmap_hbm.1, bf16[128,128]{1,0:T(8,128)(2,1)} %kmap_hbm.1), custom_call_target="tpu_custom_call" | custom-call | tf_op jit(solution)/shard_map/hedgehog/pallas_call | solution.py:426
  71.1 1.5 %slice_bitcast_fusion = (f32[128,128]{1,0:T(8,128)}, f32[128,128]{1,0:T(8,128)}) fusion(f32[2,16,8,128]{3,2,1,0:T(8,128)} %hedgehog.1), kind=kLoop, calls=%fused_computation | loop fusion | bytes 262144 | tf_op jit(solution)/shard_map/reshape;squeeze | solution.py:473

commit v7 on v6

--- a/solution.py
+++ b/solution.py
@@ -363,12 +363,12 @@
     grad_den = -jnp.sum(misfit * output, 1, keepdims=True) / denominator
     gnum = split(grad_num)
     gnum_side = side(gnum)
-    query_sum = jnp.sum(query_phi * grad_den, 0, keepdims=True)
     for sign in range(2):
         lanes = slice(sign * DH, (sign + 1) * DH)
         back = mm_wide(qphi_t[0][lanes], gnum_side) + mm(qphi_t[1][lanes], gnum[0], NN)
         state_c[sign, :, :FC, :] = back.reshape(NZ, FC, DH)
-        state_c[sign, :, FC, :] = jnp.broadcast_to(query_sum[:, lanes], (NZ, DH))
+        query_sum = jnp.sum(query_phi[:, lanes] * grad_den, 0, keepdims=True)
+        state_c[sign, :, FC, :] = jnp.broadcast_to(query_sum, (NZ, DH))
         scatter_z(1, sign)
     for sign in range(2):
         send_rows(1, sign, Z_NEAR)

time: 73.4 us -> 73.1 us (level)
  no operation moved by 1% of the time
where the time goes in v7:
time: 73.1 us; the launch traced here: 72.5 us
  Pallas kernels  70.4 us (96%)
  local copies, waits for them, and re-layouts  1.53 us (2%)
    pallas_call x1, Pallas kernels, per_device(): pl.pallas_call(kernel, out_shape=jax.ShapeDtypeStruct((2, NP, 8, DH), F32...  70.4 us
    another operation x1, local copies, waits for them, and re-layouts, per_device(): return (out[0].reshape(DH, DH), out[1].reshape(DH, DH))  1.53 us

profile of v7, /device:TPU:1, one launch (start us, length us, event | category | flops | bytes accessed | tf_op | source)
XLA Modules:
  0.0 72.5 jit_solution(8230200594536026729)
XLA Ops:
  0.6 70.4 %hedgehog.1 = f32[2,16,8,128]{3,2,1,0:T(8,128)} custom-call(bf16[512,128]{1,0:T(8,128)(2,1)} %bitcast.8, bf16[512,128]{1,0:T(8,128)(2,1)} %bitcast.9, bf16[512,128]{1,0:T(8,128)(2,1)} %bitcast.10, bf16[512,128]{1,0:T(8,128)(2,1)} %bitcast.11, bf16[128,128]{1,0:T(8,128)(2,1)} %qmap_hbm.1, bf16[128,128]{1,0:T(8,128)(2,1)} %kmap_hbm.1), custom_call_target="tpu_custom_call" | custom-call | tf_op jit(solution)/shard_map/hedgehog/pallas_call | solution.py:426
  71.0 1.5 %slice_bitcast_fusion = (f32[128,128]{1,0:T(8,128)}, f32[128,128]{1,0:T(8,128)}) fusion(f32[2,16,8,128]{3,2,1,0:T(8,128)} %hedgehog.1), kind=kLoop, calls=%fused_computation | loop fusion | bytes 262144 | tf_op jit(solution)/shard_map/reshape;squeeze | solution.py:473
